TPU v7x, 512 devices: a whole 4x4x16 slice. The times are simulated.
512 devices in a mesh: snap: 16 (over z), vert: 32 (over y, x, core).
Axes of the slice: x: 4, y: 4, z: 16, core: 2. Of those that a mesh axis runs over, the one named last changes fastest.
Arguments:
- features: bfloat16 [16, 24576, 128], P('snap', 'vert'), may hold values from -6 to 6
- adjacency_tiles: bfloat16 [16, 384, 128, 128], P('snap', 'vert'), may hold values from -0.375 to 0.375
- src_block: int32 [16, 384], P('snap', 'vert'), may hold values from 0 to 191, as said below
- dst_block: int32 [16, 384], P('snap', 'vert'), may hold values from 0 to 5
- block_count: int32 [16, 32], P('snap', 'vert'), may hold values from 6 to 12, as said below
- w_conv: bfloat16 [128, 512], replicated, may hold values from -0.5 to 0.5
- b_conv: float32 [512], replicated, may hold values from -3 to 3
- w_input: bfloat16 [512, 2048], replicated, may hold values from -0.25 to 0.25
- w_state: bfloat16 [512, 2048], replicated, may hold values from -0.25 to 0.25
- b_gates: float32 [2048], replicated, may hold values from -3 to 3
Outputs:
- hidden_seq: bfloat16 [16, 24576, 512], P('snap', 'vert')
Inputs may be any that keep to these rules, and one draw needn't show every extreme that they name: `src_block`: slot s of owner v names a column block held by owner v - 1, v or v + 1 (clipped to the owners that exist); its first slot names one of owner v - 1 and its second one of owner v + 1 where those exist. `block_count`: in every snapshot some owner has all 12 slots live.
All inputs are finite; a program needn't handle non-finite values.
Results may differ from a plain program's by a relative error of at most 0.0044.
Values may be sent and summed in bfloat16 or wider, within the bound.
A program may use at most 64 MiB of HBM per device.

v0:
```python
import jax
import jax.numpy as jnp
from jax import lax
from jax.sharding import PartitionSpec as P

FRONT = 128


forget_bias = 2.0


def padded(cells, sides, width):
    for axis, dim in sides:
        count = lax.axis_size(axis)
        ends = count - 1
        head = lax.slice_in_dim(cells, 0, width, axis=dim)
        tail = lax.slice_in_dim(cells, cells.shape[dim] - width, cells.shape[dim], axis=dim)
        cells = jnp.concatenate(
            [
                lax.ppermute(tail, axis, [(i, (i + 1) % count) for i in range(ends)]),
                cells,
                lax.ppermute(head, axis, [((i + 1) % count, i) for i in range(ends)]),
            ],
            axis=dim,
        )
    return cells


def from_behind(value, axis, steps):
    count = lax.axis_size(axis)
    initial, last = (max(0, -steps), min(count, count - steps))
    return lax.ppermute(value, axis, [(source, source + steps) for source in range(initial, last)])


def gate_step(hidden, cell, pre_gates, w_state, b_gates):
    width = w_state.shape[0]
    gates = pre_gates + jnp.dot(hidden, w_state, preferred_element_type=jnp.float32) + b_gates
    input_gate = jax.nn.sigmoid(gates[:, :width])
    forget_gate = jax.nn.sigmoid(gates[:, width : 2 * width] + forget_bias)
    candidate = jnp.tanh(gates[:, 2 * width : 3 * width])
    output_gate = jax.nn.sigmoid(gates[:, 3 * width :])
    new_cell = forget_gate * cell + input_gate * candidate
    new_hidden = (output_gate * jnp.tanh(new_cell)).astype(jnp.bfloat16)
    return (new_hidden, new_cell)


def shards(
    features,
    adjacency_tiles,
    src_block,
    dst_block,
    block_count,
    w_conv,
    b_conv,
    w_input,
    w_state,
    b_gates,
):
    vert_rows = features.shape[1]
    feat_width = features.shape[2]
    block_rows = adjacency_tiles.shape[2]
    slot_count = adjacency_tiles.shape[1]
    row_blocks = vert_rows // block_rows
    hid_width = w_state.shape[0]
    owner_index = lax.axis_index("vert")
    window = padded(features, (("vert", 1),), vert_rows)
    window_blocks = window[0].reshape(3 * row_blocks, block_rows, feat_width)
    local_index = src_block[0] - (owner_index - 1) * row_blocks
    picked = jnp.take(window_blocks, local_index, axis=0)
    product = jnp.einsum(
        "ebk,ekf->ebf", adjacency_tiles[0], picked, preferred_element_type=jnp.float32
    )
    alive = jnp.arange(slot_count, dtype=jnp.int32) < block_count[0, 0]
    selector = (
        (dst_block[0][None, :] == jnp.arange(row_blocks, dtype=jnp.int32)[:, None]) & alive[None, :]
    ).astype(jnp.float32)
    summed = jnp.einsum("re,ebf->rbf", selector, product, precision=lax.Precision.HIGHEST)
    summed = summed.reshape(vert_rows, feat_width).astype(jnp.bfloat16)
    conv = jax.nn.relu(jnp.dot(summed, w_conv, preferred_element_type=jnp.float32) + b_conv).astype(
        jnp.bfloat16
    )
    pre_gates = jnp.dot(conv, w_input, preferred_element_type=jnp.float32)
    section_index = lax.axis_index("snap")
    section_count = lax.axis_size("snap")
    front_count = vert_rows // FRONT

    def tick_body(tick_index, carry):
        out_hidden, sent_hidden, sent_cell = carry
        got_hidden = from_behind(sent_hidden, "snap", 1)
        got_cell = from_behind(sent_cell, "snap", 1)
        front_index = tick_index - section_index
        active = (front_index >= 0) & (front_index < front_count)

        def run_front(operands):
            hidden_buffer, recv_hidden, recv_cell = operands
            start_row = jnp.clip(front_index, 0, front_count - 1) * FRONT
            front_gates = lax.dynamic_slice_in_dim(pre_gates, start_row, FRONT, 0)
            new_hidden, new_cell = gate_step(recv_hidden, recv_cell, front_gates, w_state, b_gates)
            hidden_buffer = lax.dynamic_update_slice_in_dim(hidden_buffer, new_hidden, start_row, 0)
            return (hidden_buffer, new_hidden, new_cell)

        def skip_front(operands):
            return (operands[0], jnp.zeros_like(operands[1]), jnp.zeros_like(operands[2]))

        return lax.cond(active, run_front, skip_front, (out_hidden, got_hidden, got_cell))

    start_state = (
        jnp.zeros((vert_rows, hid_width), jnp.bfloat16),
        jnp.zeros((FRONT, hid_width), jnp.bfloat16),
        jnp.zeros((FRONT, hid_width), jnp.float32),
    )
    out_hidden, _, _ = lax.fori_loop(0, section_count + front_count - 1, tick_body, start_state)
    return out_hidden[None]


def solution(mesh):
    placed = (
        P("snap", "vert", None),
        P("snap", "vert", None, None),
        P("snap", "vert"),
        P("snap", "vert"),
        P("snap", "vert"),
        P(),
        P(),
        P(),
        P(),
        P(),
    )
    return jax.shard_map(
        shards, mesh=mesh, in_specs=placed, out_specs=P("snap", "vert", None), check_vma=False
    )
```

profile of v0, /device:TPU:504, one launch (start us, length us, event | category | flops | bytes accessed | tf_op | source)
XLA Modules:
  0.0 326.6 jit_solution(16320904917229424145)
XLA Ops:
  0.0 2.0 collective-permute-start.2
  2.1 5.8 %collective-permute-start.3 = (bf16[1,768,128]{2,1,0:T(8,128)(2,1)}, bf16[1,768,128]{2,1,0:T(8,128)(2,1)S(1)}, u32[]{:S(2)}, u32[]{:S(2)}) collective-permute-start(bf16[1,768,128]{2,1,0:T(8,128)(2,1)} %param.14), channel_id=1, source_target_pairs={{1,0},{2,1},{3,2},{4,3},{5,4},{6,5},{7,6},{8,7},{9,8},{10,9},{11,1... | collective-permute-start | bytes 589832 | tf_op jit(solution)/shard_map/ppermute | solution.py:22
  9.8 1.5 collective-permute-done.3
  12.9 1.4 fusion.20
  14.4 1.7 copy.12
  16.6 4.6 %fusion.16 = f32[768,2048]{1,0:T(8,128)} fusion(bf16[512,2048]{1,0:T(8,128)(2,1)S(1)} %copy-done, bf16[768,128]{1,0:T(8,128)(2,1)S(1)} %bitcast.27, bf16[128,512]{1,0:T(8,128)(2,1)S(1)} %copy-done.5, f32[512]{0:T(512)S(1)} %copy-done.6), kind=kOutput, calls=%fused_computation.24 | convolution fusion | flops 1712455680 | bytes 8718336 | tf_op jit(solution)/shard_map/dot_general | solution.py:82
  22.7 303.1 %while.20 = (s32[]{:T(128)}, bf16[768,512]{1,0:T(8,128)(2,1)S(1)}, bf16[128,512]{1,0:T(8,128)(2,1)}, f32[128,512]{1,0:T(8,128)}, s32[]{:T(128)}, /*index=5*/f32[...) while((s32[]{:T(128)}, bf16[768,512]{1,0:T(8,128)(2,1)S(1)}, ...), condition=%wide.region_3.4_spmd, body=%wide.region_0.3_spmd.sunk | while | flops 269942784 | bytes 7741817 | solution.py:112
  25.3 10.1 %collective-permute-done = bf16[128,512]{1,0:T(8,128)(2,1)S(1)} collective-permute-done((bf16[128,512]{1,0:T(8,128)(2,1)}, bf16[128,512]{1,0:T(8,128)(2,1)S(1)}, u32[]{:S(2)}, u32[]{:S(2)}) %collective-permute-start) | collective-permute-done | bytes 131104 | tf_op jit(solution)/shard_map/while/body/eval_jaxpr/ppermute | solution.py:32
  35.4 1.4 conditional.2
  39.4 9.2 %collective-permute-done = bf16[128,512]{1,0:T(8,128)(2,1)S(1)} collective-permute-done((bf16[128,512]{1,0:T(8,128)(2,1)}, bf16[128,512]{1,0:T(8,128)(2,1)S(1)}, u32[]{:S(2)}, u32[]{:S(2)}) %collective-permute-start) | collective-permute-done | bytes 131104 | tf_op jit(solution)/shard_map/while/body/eval_jaxpr/ppermute | solution.py:32
  48.5 1.4 conditional.2
  52.5 8.2 %collective-permute-done = bf16[128,512]{1,0:T(8,128)(2,1)S(1)} collective-permute-done((bf16[128,512]{1,0:T(8,128)(2,1)}, bf16[128,512]{1,0:T(8,128)(2,1)S(1)}, u32[]{:S(2)}, u32[]{:S(2)}) %collective-permute-start) | collective-permute-done | bytes 131104 | tf_op jit(solution)/shard_map/while/body/eval_jaxpr/ppermute | solution.py:32
  60.7 1.4 conditional.2
  64.7 7.3 %collective-permute-done = bf16[128,512]{1,0:T(8,128)(2,1)S(1)} collective-permute-done((bf16[128,512]{1,0:T(8,128)(2,1)}, bf16[128,512]{1,0:T(8,128)(2,1)S(1)}, u32[]{:S(2)}, u32[]{:S(2)}) %collective-permute-start) | collective-permute-done | bytes 131104 | tf_op jit(solution)/shard_map/while/body/eval_jaxpr/ppermute | solution.py:32
  72.0 1.4 conditional.2
  76.0 7.5 %collective-permute-done = bf16[128,512]{1,0:T(8,128)(2,1)S(1)} collective-permute-done((bf16[128,512]{1,0:T(8,128)(2,1)}, bf16[128,512]{1,0:T(8,128)(2,1)S(1)}, u32[]{:S(2)}, u32[]{:S(2)}) %collective-permute-start) | collective-permute-done | bytes 131104 | tf_op jit(solution)/shard_map/while/body/eval_jaxpr/ppermute | solution.py:32
  83.5 1.4 conditional.2
  87.5 7.9 %collective-permute-done = bf16[128,512]{1,0:T(8,128)(2,1)S(1)} collective-permute-done((bf16[128,512]{1,0:T(8,128)(2,1)}, bf16[128,512]{1,0:T(8,128)(2,1)S(1)}, u32[]{:S(2)}, u32[]{:S(2)}) %collective-permute-start) | collective-permute-done | bytes 131104 | tf_op jit(solution)/shard_map/while/body/eval_jaxpr/ppermute | solution.py:32
  95.4 1.4 conditional.2
  99.4 8.2 %collective-permute-done = bf16[128,512]{1,0:T(8,128)(2,1)S(1)} collective-permute-done((bf16[128,512]{1,0:T(8,128)(2,1)}, bf16[128,512]{1,0:T(8,128)(2,1)S(1)}, u32[]{:S(2)}, u32[]{:S(2)}) %collective-permute-start) | collective-permute-done | bytes 131104 | tf_op jit(solution)/shard_map/while/body/eval_jaxpr/ppermute | solution.py:32
  107.6 1.4 conditional.2
  111.6 9.3 %collective-permute-done = bf16[128,512]{1,0:T(8,128)(2,1)S(1)} collective-permute-done((bf16[128,512]{1,0:T(8,128)(2,1)}, bf16[128,512]{1,0:T(8,128)(2,1)S(1)}, u32[]{:S(2)}, u32[]{:S(2)}) %collective-permute-start) | collective-permute-done | bytes 131104 | tf_op jit(solution)/shard_map/while/body/eval_jaxpr/ppermute | solution.py:32
  120.9 1.4 conditional.2
  124.9 10.7 %collective-permute-done = bf16[128,512]{1,0:T(8,128)(2,1)S(1)} collective-permute-done((bf16[128,512]{1,0:T(8,128)(2,1)}, bf16[128,512]{1,0:T(8,128)(2,1)S(1)}, u32[]{:S(2)}, u32[]{:S(2)}) %collective-permute-start) | collective-permute-done | bytes 131104 | tf_op jit(solution)/shard_map/while/body/eval_jaxpr/ppermute | solution.py:32
  139.5 12.3 %collective-permute-done = bf16[128,512]{1,0:T(8,128)(2,1)S(1)} collective-permute-done((bf16[128,512]{1,0:T(8,128)(2,1)}, bf16[128,512]{1,0:T(8,128)(2,1)S(1)}, u32[]{:S(2)}, u32[]{:S(2)}) %collective-permute-start) | collective-permute-done | bytes 131104 | tf_op jit(solution)/shard_map/while/body/eval_jaxpr/ppermute | solution.py:32
  155.8 13.5 %collective-permute-done = bf16[128,512]{1,0:T(8,128)(2,1)S(1)} collective-permute-done((bf16[128,512]{1,0:T(8,128)(2,1)}, bf16[128,512]{1,0:T(8,128)(2,1)S(1)}, u32[]{:S(2)}, u32[]{:S(2)}) %collective-permute-start) | collective-permute-done | bytes 131104 | tf_op jit(solution)/shard_map/while/body/eval_jaxpr/ppermute | solution.py:32
  173.3 12.4 %collective-permute-done = bf16[128,512]{1,0:T(8,128)(2,1)S(1)} collective-permute-done((bf16[128,512]{1,0:T(8,128)(2,1)}, bf16[128,512]{1,0:T(8,128)(2,1)S(1)}, u32[]{:S(2)}, u32[]{:S(2)}) %collective-permute-start) | collective-permute-done | bytes 131104 | tf_op jit(solution)/shard_map/while/body/eval_jaxpr/ppermute | solution.py:32
  189.6 10.8 %collective-permute-done = bf16[128,512]{1,0:T(8,128)(2,1)S(1)} collective-permute-done((bf16[128,512]{1,0:T(8,128)(2,1)}, bf16[128,512]{1,0:T(8,128)(2,1)S(1)}, u32[]{:S(2)}, u32[]{:S(2)}) %collective-permute-start) | collective-permute-done | bytes 131104 | tf_op jit(solution)/shard_map/while/body/eval_jaxpr/ppermute | solution.py:32
  204.4 9.1 %collective-permute-done = bf16[128,512]{1,0:T(8,128)(2,1)S(1)} collective-permute-done((bf16[128,512]{1,0:T(8,128)(2,1)}, bf16[128,512]{1,0:T(8,128)(2,1)S(1)}, u32[]{:S(2)}, u32[]{:S(2)}) %collective-permute-start) | collective-permute-done | bytes 131104 | tf_op jit(solution)/shard_map/while/body/eval_jaxpr/ppermute | solution.py:32
  217.5 13.3 %collective-permute-done = bf16[128,512]{1,0:T(8,128)(2,1)S(1)} collective-permute-done((bf16[128,512]{1,0:T(8,128)(2,1)}, bf16[128,512]{1,0:T(8,128)(2,1)S(1)}, u32[]{:S(2)}, u32[]{:S(2)}) %collective-permute-start) | collective-permute-done | bytes 131104 | tf_op jit(solution)/shard_map/while/body/eval_jaxpr/ppermute | solution.py:32
  234.7 16.4 %collective-permute-done = bf16[128,512]{1,0:T(8,128)(2,1)S(1)} collective-permute-done((bf16[128,512]{1,0:T(8,128)(2,1)}, bf16[128,512]{1,0:T(8,128)(2,1)S(1)}, u32[]{:S(2)}, u32[]{:S(2)}) %collective-permute-start) | collective-permute-done | bytes 131104 | tf_op jit(solution)/shard_map/while/body/eval_jaxpr/ppermute | solution.py:32
  251.1 3.3 %conditional.2 = ((bf16[768,512]{1,0:T(8,128)(2,1)S(1)}, bf16[128,512]{1,0:T(8,128)(2,1)}, f32[128,512]{1,0:T(8,128)})) conditional(s32[]{:T(128)} %convert_element_type.30, bf16[768,512]{1,0:T(8,128)(2,1)S(1)} %get-tuple-element.268, (s32[]{:T(128)}, f32[768,2048]{1,0:T(8,128)}, bf16[128,512]{1,0:T(8,128)(2,1)S(1)}, bf16[512,2048]{1,0:T(8,128)(2,1)}, ...), branch_computations={%region_1.1_spmd, %region_2.2_spmd} | conditional | flops 269942784 | bytes 6168662 | solution.py:105
  251.1 2.3 fusion
  257.0 8.4 %collective-permute-done = bf16[128,512]{1,0:T(8,128)(2,1)S(1)} collective-permute-done((bf16[128,512]{1,0:T(8,128)(2,1)}, bf16[128,512]{1,0:T(8,128)(2,1)S(1)}, u32[]{:S(2)}, u32[]{:S(2)}) %collective-permute-start) | collective-permute-done | bytes 131104 | tf_op jit(solution)/shard_map/while/body/eval_jaxpr/ppermute | solution.py:32
  265.5 3.3 %conditional.2 = ((bf16[768,512]{1,0:T(8,128)(2,1)S(1)}, bf16[128,512]{1,0:T(8,128)(2,1)}, f32[128,512]{1,0:T(8,128)})) conditional(s32[]{:T(128)} %convert_element_type.30, bf16[768,512]{1,0:T(8,128)(2,1)S(1)} %get-tuple-element.268, (s32[]{:T(128)}, f32[768,2048]{1,0:T(8,128)}, bf16[128,512]{1,0:T(8,128)(2,1)S(1)}, bf16[512,2048]{1,0:T(8,128)(2,1)}, ...), branch_computations={%region_1.1_spmd, %region_2.2_spmd} | conditional | flops 269942784 | bytes 6168662 | solution.py:105
  265.5 2.3 fusion
  271.4 7.6 %collective-permute-done = bf16[128,512]{1,0:T(8,128)(2,1)S(1)} collective-permute-done((bf16[128,512]{1,0:T(8,128)(2,1)}, bf16[128,512]{1,0:T(8,128)(2,1)S(1)}, u32[]{:S(2)}, u32[]{:S(2)}) %collective-permute-start) | collective-permute-done | bytes 131104 | tf_op jit(solution)/shard_map/while/body/eval_jaxpr/ppermute | solution.py:32
  279.0 3.3 %conditional.2 = ((bf16[768,512]{1,0:T(8,128)(2,1)S(1)}, bf16[128,512]{1,0:T(8,128)(2,1)}, f32[128,512]{1,0:T(8,128)})) conditional(s32[]{:T(128)} %convert_element_type.30, bf16[768,512]{1,0:T(8,128)(2,1)S(1)} %get-tuple-element.268, (s32[]{:T(128)}, f32[768,2048]{1,0:T(8,128)}, bf16[128,512]{1,0:T(8,128)(2,1)S(1)}, bf16[512,2048]{1,0:T(8,128)(2,1)}, ...), branch_computations={%region_1.1_spmd, %region_2.2_spmd} | conditional | flops 269942784 | bytes 6168662 | solution.py:105
  279.0 2.3 fusion
  285.0 7.9 %collective-permute-done = bf16[128,512]{1,0:T(8,128)(2,1)S(1)} collective-permute-done((bf16[128,512]{1,0:T(8,128)(2,1)}, bf16[128,512]{1,0:T(8,128)(2,1)S(1)}, u32[]{:S(2)}, u32[]{:S(2)}) %collective-permute-start) | collective-permute-done | bytes 131104 | tf_op jit(solution)/shard_map/while/body/eval_jaxpr/ppermute | solution.py:32
  292.9 3.3 %conditional.2 = ((bf16[768,512]{1,0:T(8,128)(2,1)S(1)}, bf16[128,512]{1,0:T(8,128)(2,1)}, f32[128,512]{1,0:T(8,128)})) conditional(s32[]{:T(128)} %convert_element_type.30, bf16[768,512]{1,0:T(8,128)(2,1)S(1)} %get-tuple-element.268, (s32[]{:T(128)}, f32[768,2048]{1,0:T(8,128)}, bf16[128,512]{1,0:T(8,128)(2,1)S(1)}, bf16[512,2048]{1,0:T(8,128)(2,1)}, ...), branch_computations={%region_1.1_spmd, %region_2.2_spmd} | conditional | flops 269942784 | bytes 6168662 | solution.py:105
  292.9 2.3 fusion
  298.8 8.2 %collective-permute-done = bf16[128,512]{1,0:T(8,128)(2,1)S(1)} collective-permute-done((bf16[128,512]{1,0:T(8,128)(2,1)}, bf16[128,512]{1,0:T(8,128)(2,1)S(1)}, u32[]{:S(2)}, u32[]{:S(2)}) %collective-permute-start) | collective-permute-done | bytes 131104 | tf_op jit(solution)/shard_map/while/body/eval_jaxpr/ppermute | solution.py:32
  307.0 3.3 %conditional.2 = ((bf16[768,512]{1,0:T(8,128)(2,1)S(1)}, bf16[128,512]{1,0:T(8,128)(2,1)}, f32[128,512]{1,0:T(8,128)})) conditional(s32[]{:T(128)} %convert_element_type.30, bf16[768,512]{1,0:T(8,128)(2,1)S(1)} %get-tuple-element.268, (s32[]{:T(128)}, f32[768,2048]{1,0:T(8,128)}, bf16[128,512]{1,0:T(8,128)(2,1)S(1)}, bf16[512,2048]{1,0:T(8,128)(2,1)}, ...), branch_computations={%region_1.1_spmd, %region_2.2_spmd} | conditional | flops 269942784 | bytes 6168662 | solution.py:105
  307.0 2.3 fusion
  312.9 9.5 %collective-permute-done = bf16[128,512]{1,0:T(8,128)(2,1)S(1)} collective-permute-done((bf16[128,512]{1,0:T(8,128)(2,1)}, bf16[128,512]{1,0:T(8,128)(2,1)S(1)}, u32[]{:S(2)}, u32[]{:S(2)}) %collective-permute-start) | collective-permute-done | bytes 131104 | tf_op jit(solution)/shard_map/while/body/eval_jaxpr/ppermute | solution.py:32
  322.4 3.3 %conditional.2 = ((bf16[768,512]{1,0:T(8,128)(2,1)S(1)}, bf16[128,512]{1,0:T(8,128)(2,1)}, f32[128,512]{1,0:T(8,128)})) conditional(s32[]{:T(128)} %convert_element_type.30, bf16[768,512]{1,0:T(8,128)(2,1)S(1)} %get-tuple-element.268, (s32[]{:T(128)}, f32[768,2048]{1,0:T(8,128)}, bf16[128,512]{1,0:T(8,128)(2,1)S(1)}, bf16[512,2048]{1,0:T(8,128)(2,1)}, ...), branch_computations={%region_1.1_spmd, %region_2.2_spmd} | conditional | flops 269942784 | bytes 6168662 | solution.py:105
  322.4 2.3 fusion
  (132 shorter events, 96.3 us)
Async XLA Ops:
  0.0 16.6 %copy-start = (bf16[512,2048]{1,0:T(8,128)(2,1)S(1)}, bf16[512,2048]{1,0:T(8,128)(2,1)}, u32[]{:S(2)}) copy-start(bf16[512,2048]{1,0:T(8,128)(2,1)} %param.21) | copy-start | bytes 6291460
  0.0 12.9 %copy-start.2 = (bf16[1,12,128,128]{3,2,1,0:T(8,128)(2,1)S(1)}, bf16[1,12,128,128]{3,2,1,0:T(8,128)(2,1)}, u32[]{:S(2)}) copy-start(bf16[1,12,128,128]{3,2,1,0:T(8,128)(2,1)} %param.15) | copy-start | bytes 1179652
  0.0 9.8 %collective-permute-start.2 = (bf16[1,768,128]{2,1,0:T(8,128)(2,1)}, bf16[1,768,128]{2,1,0:T(8,128)(2,1)S(1)}, u32[]{:S(2)}, u32[]{:S(2)}) collective-permute-start(bf16[1,768,128]{2,1,0:T(8,128)(2,1)} %param.14), channel_id=1, source_target_pairs={{0,1},{1,2},{2,3},{3,4},{4,5},{5,6},{6,7},{7,8},{8,9},{9,10},{10,1... | collective-permute-start | bytes 589832 | tf_op jit(solution)/shard_map/ppermute | solution.py:20
  2.1 9.2 %collective-permute-start.3 = (bf16[1,768,128]{2,1,0:T(8,128)(2,1)}, bf16[1,768,128]{2,1,0:T(8,128)(2,1)S(1)}, u32[]{:S(2)}, u32[]{:S(2)}) collective-permute-start(bf16[1,768,128]{2,1,0:T(8,128)(2,1)} %param.14), channel_id=1, source_target_pairs={{1,0},{2,1},{3,2},{4,3},{5,4},{6,5},{7,6},{8,7},{9,8},{10,9},{11,1... | collective-permute-start | bytes 589832 | tf_op jit(solution)/shard_map/ppermute | solution.py:22
  12.3 3.8 %copy-start.4 = (s32[1,12]{1,0:T(1,128)S(1)}, s32[1,12]{1,0:T(1,128)}, u32[]{:S(2)}) copy-start(s32[1,12]{1,0:T(1,128)} %param.17) | copy-start | bytes 148
  16.6 6.1 %copy-start.3 = (f32[2048]{0:T(1024)S(1)}, f32[2048]{0:T(1024)}, u32[]{:S(2)}) copy-start(f32[2048]{0:T(1024)} %param.23) | copy-start | bytes 24580
  22.7 12.7 %collective-permute-start.1 = (f32[128,512]{1,0:T(8,128)}, f32[128,512]{1,0:T(8,128)S(1)}, u32[]{:S(2)}, u32[]{:S(2)}) collective-permute-start(f32[128,512]{1,0:T(8,128)} %get-tuple-element.270), channel_id=1, source_target_pairs={{0,32},{32,64},{64,96},{96,128},{128,160},{160,192},{192,224},{224... | collective-permute-start | bytes 786440 | tf_op jit(solution)/shard_map/while/body/eval_jaxpr/ppermute | solution.py:32
  24.0 11.4 %collective-permute-start = (bf16[128,512]{1,0:T(8,128)(2,1)}, bf16[128,512]{1,0:T(8,128)(2,1)S(1)}, u32[]{:S(2)}, u32[]{:S(2)}) collective-permute-start(bf16[128,512]{1,0:T(8,128)(2,1)} %get-tuple-element.269), channel_id=1, source_target_pairs={{0,32},{32,64},{64,96},{96,128},{128,160},{160,192},{192,224},{224... | collective-permute-start | bytes 393224 | tf_op jit(solution)/shard_map/while/body/eval_jaxpr/ppermute | solution.py:32
  36.8 11.8 %collective-permute-start.1 = (f32[128,512]{1,0:T(8,128)}, f32[128,512]{1,0:T(8,128)S(1)}, u32[]{:S(2)}, u32[]{:S(2)}) collective-permute-start(f32[128,512]{1,0:T(8,128)} %get-tuple-element.270), channel_id=1, source_target_pairs={{0,32},{32,64},{64,96},{96,128},{128,160},{160,192},{192,224},{224... | collective-permute-start | bytes 786440 | tf_op jit(solution)/shard_map/while/body/eval_jaxpr/ppermute | solution.py:32
  38.0 10.5 %collective-permute-start = (bf16[128,512]{1,0:T(8,128)(2,1)}, bf16[128,512]{1,0:T(8,128)(2,1)S(1)}, u32[]{:S(2)}, u32[]{:S(2)}) collective-permute-start(bf16[128,512]{1,0:T(8,128)(2,1)} %get-tuple-element.269), channel_id=1, source_target_pairs={{0,32},{32,64},{64,96},{96,128},{128,160},{160,192},{192,224},{224... | collective-permute-start | bytes 393224 | tf_op jit(solution)/shard_map/while/body/eval_jaxpr/ppermute | solution.py:32
  49.9 10.8 %collective-permute-start.1 = (f32[128,512]{1,0:T(8,128)}, f32[128,512]{1,0:T(8,128)S(1)}, u32[]{:S(2)}, u32[]{:S(2)}) collective-permute-start(f32[128,512]{1,0:T(8,128)} %get-tuple-element.270), channel_id=1, source_target_pairs={{0,32},{32,64},{64,96},{96,128},{128,160},{160,192},{192,224},{224... | collective-permute-start | bytes 786440 | tf_op jit(solution)/shard_map/while/body/eval_jaxpr/ppermute | solution.py:32
  51.2 9.5 %collective-permute-start = (bf16[128,512]{1,0:T(8,128)(2,1)}, bf16[128,512]{1,0:T(8,128)(2,1)S(1)}, u32[]{:S(2)}, u32[]{:S(2)}) collective-permute-start(bf16[128,512]{1,0:T(8,128)(2,1)} %get-tuple-element.269), channel_id=1, source_target_pairs={{0,32},{32,64},{64,96},{96,128},{128,160},{160,192},{192,224},{224... | collective-permute-start | bytes 393224 | tf_op jit(solution)/shard_map/while/body/eval_jaxpr/ppermute | solution.py:32
  62.1 9.9 %collective-permute-start.1 = (f32[128,512]{1,0:T(8,128)}, f32[128,512]{1,0:T(8,128)S(1)}, u32[]{:S(2)}, u32[]{:S(2)}) collective-permute-start(f32[128,512]{1,0:T(8,128)} %get-tuple-element.270), channel_id=1, source_target_pairs={{0,32},{32,64},{64,96},{96,128},{128,160},{160,192},{192,224},{224... | collective-permute-start | bytes 786440 | tf_op jit(solution)/shard_map/while/body/eval_jaxpr/ppermute | solution.py:32
  63.4 8.6 %collective-permute-start = (bf16[128,512]{1,0:T(8,128)(2,1)}, bf16[128,512]{1,0:T(8,128)(2,1)S(1)}, u32[]{:S(2)}, u32[]{:S(2)}) collective-permute-start(bf16[128,512]{1,0:T(8,128)(2,1)} %get-tuple-element.269), channel_id=1, source_target_pairs={{0,32},{32,64},{64,96},{96,128},{128,160},{160,192},{192,224},{224... | collective-permute-start | bytes 393224 | tf_op jit(solution)/shard_map/while/body/eval_jaxpr/ppermute | solution.py:32
  73.4 10.1 %collective-permute-start.1 = (f32[128,512]{1,0:T(8,128)}, f32[128,512]{1,0:T(8,128)S(1)}, u32[]{:S(2)}, u32[]{:S(2)}) collective-permute-start(f32[128,512]{1,0:T(8,128)} %get-tuple-element.270), channel_id=1, source_target_pairs={{0,32},{32,64},{64,96},{96,128},{128,160},{160,192},{192,224},{224... | collective-permute-start | bytes 786440 | tf_op jit(solution)/shard_map/while/body/eval_jaxpr/ppermute | solution.py:32
  74.7 8.8 %collective-permute-start = (bf16[128,512]{1,0:T(8,128)(2,1)}, bf16[128,512]{1,0:T(8,128)(2,1)S(1)}, u32[]{:S(2)}, u32[]{:S(2)}) collective-permute-start(bf16[128,512]{1,0:T(8,128)(2,1)} %get-tuple-element.269), channel_id=1, source_target_pairs={{0,32},{32,64},{64,96},{96,128},{128,160},{160,192},{192,224},{224... | collective-permute-start | bytes 393224 | tf_op jit(solution)/shard_map/while/body/eval_jaxpr/ppermute | solution.py:32
  84.9 10.5 %collective-permute-start.1 = (f32[128,512]{1,0:T(8,128)}, f32[128,512]{1,0:T(8,128)S(1)}, u32[]{:S(2)}, u32[]{:S(2)}) collective-permute-start(f32[128,512]{1,0:T(8,128)} %get-tuple-element.270), channel_id=1, source_target_pairs={{0,32},{32,64},{64,96},{96,128},{128,160},{160,192},{192,224},{224... | collective-permute-start | bytes 786440 | tf_op jit(solution)/shard_map/while/body/eval_jaxpr/ppermute | solution.py:32
  86.2 9.2 %collective-permute-start = (bf16[128,512]{1,0:T(8,128)(2,1)}, bf16[128,512]{1,0:T(8,128)(2,1)S(1)}, u32[]{:S(2)}, u32[]{:S(2)}) collective-permute-start(bf16[128,512]{1,0:T(8,128)(2,1)} %get-tuple-element.269), channel_id=1, source_target_pairs={{0,32},{32,64},{64,96},{96,128},{128,160},{160,192},{192,224},{224... | collective-permute-start | bytes 393224 | tf_op jit(solution)/shard_map/while/body/eval_jaxpr/ppermute | solution.py:32
  96.8 10.8 %collective-permute-start.1 = (f32[128,512]{1,0:T(8,128)}, f32[128,512]{1,0:T(8,128)S(1)}, u32[]{:S(2)}, u32[]{:S(2)}) collective-permute-start(f32[128,512]{1,0:T(8,128)} %get-tuple-element.270), channel_id=1, source_target_pairs={{0,32},{32,64},{64,96},{96,128},{128,160},{160,192},{192,224},{224... | collective-permute-start | bytes 786440 | tf_op jit(solution)/shard_map/while/body/eval_jaxpr/ppermute | solution.py:32
  98.1 9.5 %collective-permute-start = (bf16[128,512]{1,0:T(8,128)(2,1)}, bf16[128,512]{1,0:T(8,128)(2,1)S(1)}, u32[]{:S(2)}, u32[]{:S(2)}) collective-permute-start(bf16[128,512]{1,0:T(8,128)(2,1)} %get-tuple-element.269), channel_id=1, source_target_pairs={{0,32},{32,64},{64,96},{96,128},{128,160},{160,192},{192,224},{224... | collective-permute-start | bytes 393224 | tf_op jit(solution)/shard_map/while/body/eval_jaxpr/ppermute | solution.py:32
  109.0 11.9 %collective-permute-start.1 = (f32[128,512]{1,0:T(8,128)}, f32[128,512]{1,0:T(8,128)S(1)}, u32[]{:S(2)}, u32[]{:S(2)}) collective-permute-start(f32[128,512]{1,0:T(8,128)} %get-tuple-element.270), channel_id=1, source_target_pairs={{0,32},{32,64},{64,96},{96,128},{128,160},{160,192},{192,224},{224... | collective-permute-start | bytes 786440 | tf_op jit(solution)/shard_map/while/body/eval_jaxpr/ppermute | solution.py:32
  110.3 10.6 %collective-permute-start = (bf16[128,512]{1,0:T(8,128)(2,1)}, bf16[128,512]{1,0:T(8,128)(2,1)S(1)}, u32[]{:S(2)}, u32[]{:S(2)}) collective-permute-start(bf16[128,512]{1,0:T(8,128)(2,1)} %get-tuple-element.269), channel_id=1, source_target_pairs={{0,32},{32,64},{64,96},{96,128},{128,160},{160,192},{192,224},{224... | collective-permute-start | bytes 393224 | tf_op jit(solution)/shard_map/while/body/eval_jaxpr/ppermute | solution.py:32
  122.3 13.3 %collective-permute-start.1 = (f32[128,512]{1,0:T(8,128)}, f32[128,512]{1,0:T(8,128)S(1)}, u32[]{:S(2)}, u32[]{:S(2)}) collective-permute-start(f32[128,512]{1,0:T(8,128)} %get-tuple-element.270), channel_id=1, source_target_pairs={{0,32},{32,64},{64,96},{96,128},{128,160},{160,192},{192,224},{224... | collective-permute-start | bytes 786440 | tf_op jit(solution)/shard_map/while/body/eval_jaxpr/ppermute | solution.py:32
  123.5 12.0 %collective-permute-start = (bf16[128,512]{1,0:T(8,128)(2,1)}, bf16[128,512]{1,0:T(8,128)(2,1)S(1)}, u32[]{:S(2)}, u32[]{:S(2)}) collective-permute-start(bf16[128,512]{1,0:T(8,128)(2,1)} %get-tuple-element.269), channel_id=1, source_target_pairs={{0,32},{32,64},{64,96},{96,128},{128,160},{160,192},{192,224},{224... | collective-permute-start | bytes 393224 | tf_op jit(solution)/shard_map/while/body/eval_jaxpr/ppermute | solution.py:32
  136.9 14.9 %collective-permute-start.1 = (f32[128,512]{1,0:T(8,128)}, f32[128,512]{1,0:T(8,128)S(1)}, u32[]{:S(2)}, u32[]{:S(2)}) collective-permute-start(f32[128,512]{1,0:T(8,128)} %get-tuple-element.270), channel_id=1, source_target_pairs={{0,32},{32,64},{64,96},{96,128},{128,160},{160,192},{192,224},{224... | collective-permute-start | bytes 786440 | tf_op jit(solution)/shard_map/while/body/eval_jaxpr/ppermute | solution.py:32
  138.2 13.6 %collective-permute-start = (bf16[128,512]{1,0:T(8,128)(2,1)}, bf16[128,512]{1,0:T(8,128)(2,1)S(1)}, u32[]{:S(2)}, u32[]{:S(2)}) collective-permute-start(bf16[128,512]{1,0:T(8,128)(2,1)} %get-tuple-element.269), channel_id=1, source_target_pairs={{0,32},{32,64},{64,96},{96,128},{128,160},{160,192},{192,224},{224... | collective-permute-start | bytes 393224 | tf_op jit(solution)/shard_map/while/body/eval_jaxpr/ppermute | solution.py:32
  153.2 16.1 %collective-permute-start.1 = (f32[128,512]{1,0:T(8,128)}, f32[128,512]{1,0:T(8,128)S(1)}, u32[]{:S(2)}, u32[]{:S(2)}) collective-permute-start(f32[128,512]{1,0:T(8,128)} %get-tuple-element.270), channel_id=1, source_target_pairs={{0,32},{32,64},{64,96},{96,128},{128,160},{160,192},{192,224},{224... | collective-permute-start | bytes 786440 | tf_op jit(solution)/shard_map/while/body/eval_jaxpr/ppermute | solution.py:32
  154.5 14.8 %collective-permute-start = (bf16[128,512]{1,0:T(8,128)(2,1)}, bf16[128,512]{1,0:T(8,128)(2,1)S(1)}, u32[]{:S(2)}, u32[]{:S(2)}) collective-permute-start(bf16[128,512]{1,0:T(8,128)(2,1)} %get-tuple-element.269), channel_id=1, source_target_pairs={{0,32},{32,64},{64,96},{96,128},{128,160},{160,192},{192,224},{224... | collective-permute-start | bytes 393224 | tf_op jit(solution)/shard_map/while/body/eval_jaxpr/ppermute | solution.py:32
  170.7 15.0 %collective-permute-start.1 = (f32[128,512]{1,0:T(8,128)}, f32[128,512]{1,0:T(8,128)S(1)}, u32[]{:S(2)}, u32[]{:S(2)}) collective-permute-start(f32[128,512]{1,0:T(8,128)} %get-tuple-element.270), channel_id=1, source_target_pairs={{0,32},{32,64},{64,96},{96,128},{128,160},{160,192},{192,224},{224... | collective-permute-start | bytes 786440 | tf_op jit(solution)/shard_map/while/body/eval_jaxpr/ppermute | solution.py:32
  171.9 13.7 %collective-permute-start = (bf16[128,512]{1,0:T(8,128)(2,1)}, bf16[128,512]{1,0:T(8,128)(2,1)S(1)}, u32[]{:S(2)}, u32[]{:S(2)}) collective-permute-start(bf16[128,512]{1,0:T(8,128)(2,1)} %get-tuple-element.269), channel_id=1, source_target_pairs={{0,32},{32,64},{64,96},{96,128},{128,160},{160,192},{192,224},{224... | collective-permute-start | bytes 393224 | tf_op jit(solution)/shard_map/while/body/eval_jaxpr/ppermute | solution.py:32
  187.0 13.4 %collective-permute-start.1 = (f32[128,512]{1,0:T(8,128)}, f32[128,512]{1,0:T(8,128)S(1)}, u32[]{:S(2)}, u32[]{:S(2)}) collective-permute-start(f32[128,512]{1,0:T(8,128)} %get-tuple-element.270), channel_id=1, source_target_pairs={{0,32},{32,64},{64,96},{96,128},{128,160},{160,192},{192,224},{224... | collective-permute-start | bytes 786440 | tf_op jit(solution)/shard_map/while/body/eval_jaxpr/ppermute | solution.py:32
  188.3 12.1 %collective-permute-start = (bf16[128,512]{1,0:T(8,128)(2,1)}, bf16[128,512]{1,0:T(8,128)(2,1)S(1)}, u32[]{:S(2)}, u32[]{:S(2)}) collective-permute-start(bf16[128,512]{1,0:T(8,128)(2,1)} %get-tuple-element.269), channel_id=1, source_target_pairs={{0,32},{32,64},{64,96},{96,128},{128,160},{160,192},{192,224},{224... | collective-permute-start | bytes 393224 | tf_op jit(solution)/shard_map/while/body/eval_jaxpr/ppermute | solution.py:32
  201.8 11.7 %collective-permute-start.1 = (f32[128,512]{1,0:T(8,128)}, f32[128,512]{1,0:T(8,128)S(1)}, u32[]{:S(2)}, u32[]{:S(2)}) collective-permute-start(f32[128,512]{1,0:T(8,128)} %get-tuple-element.270), channel_id=1, source_target_pairs={{0,32},{32,64},{64,96},{96,128},{128,160},{160,192},{192,224},{224... | collective-permute-start | bytes 786440 | tf_op jit(solution)/shard_map/while/body/eval_jaxpr/ppermute | solution.py:32
  203.1 10.4 %collective-permute-start = (bf16[128,512]{1,0:T(8,128)(2,1)}, bf16[128,512]{1,0:T(8,128)(2,1)S(1)}, u32[]{:S(2)}, u32[]{:S(2)}) collective-permute-start(bf16[128,512]{1,0:T(8,128)(2,1)} %get-tuple-element.269), channel_id=1, source_target_pairs={{0,32},{32,64},{64,96},{96,128},{128,160},{160,192},{192,224},{224... | collective-permute-start | bytes 393224 | tf_op jit(solution)/shard_map/while/body/eval_jaxpr/ppermute | solution.py:32
  214.9 15.9 %collective-permute-start.1 = (f32[128,512]{1,0:T(8,128)}, f32[128,512]{1,0:T(8,128)S(1)}, u32[]{:S(2)}, u32[]{:S(2)}) collective-permute-start(f32[128,512]{1,0:T(8,128)} %get-tuple-element.270), channel_id=1, source_target_pairs={{0,32},{32,64},{64,96},{96,128},{128,160},{160,192},{192,224},{224... | collective-permute-start | bytes 786440 | tf_op jit(solution)/shard_map/while/body/eval_jaxpr/ppermute | solution.py:32
  216.2 14.6 %collective-permute-start = (bf16[128,512]{1,0:T(8,128)(2,1)}, bf16[128,512]{1,0:T(8,128)(2,1)S(1)}, u32[]{:S(2)}, u32[]{:S(2)}) collective-permute-start(bf16[128,512]{1,0:T(8,128)(2,1)} %get-tuple-element.269), channel_id=1, source_target_pairs={{0,32},{32,64},{64,96},{96,128},{128,160},{160,192},{192,224},{224... | collective-permute-start | bytes 393224 | tf_op jit(solution)/shard_map/while/body/eval_jaxpr/ppermute | solution.py:32
  232.1 19.0 %collective-permute-start.1 = (f32[128,512]{1,0:T(8,128)}, f32[128,512]{1,0:T(8,128)S(1)}, u32[]{:S(2)}, u32[]{:S(2)}) collective-permute-start(f32[128,512]{1,0:T(8,128)} %get-tuple-element.270), channel_id=1, source_target_pairs={{0,32},{32,64},{64,96},{96,128},{128,160},{160,192},{192,224},{224... | collective-permute-start | bytes 786440 | tf_op jit(solution)/shard_map/while/body/eval_jaxpr/ppermute | solution.py:32
  233.4 17.7 %collective-permute-start = (bf16[128,512]{1,0:T(8,128)(2,1)}, bf16[128,512]{1,0:T(8,128)(2,1)S(1)}, u32[]{:S(2)}, u32[]{:S(2)}) collective-permute-start(bf16[128,512]{1,0:T(8,128)(2,1)} %get-tuple-element.269), channel_id=1, source_target_pairs={{0,32},{32,64},{64,96},{96,128},{128,160},{160,192},{192,224},{224... | collective-permute-start | bytes 393224 | tf_op jit(solution)/shard_map/while/body/eval_jaxpr/ppermute | solution.py:32
  254.4 11.0 %collective-permute-start.1 = (f32[128,512]{1,0:T(8,128)}, f32[128,512]{1,0:T(8,128)S(1)}, u32[]{:S(2)}, u32[]{:S(2)}) collective-permute-start(f32[128,512]{1,0:T(8,128)} %get-tuple-element.270), channel_id=1, source_target_pairs={{0,32},{32,64},{64,96},{96,128},{128,160},{160,192},{192,224},{224... | collective-permute-start | bytes 786440 | tf_op jit(solution)/shard_map/while/body/eval_jaxpr/ppermute | solution.py:32
  255.7 9.7 %collective-permute-start = (bf16[128,512]{1,0:T(8,128)(2,1)}, bf16[128,512]{1,0:T(8,128)(2,1)S(1)}, u32[]{:S(2)}, u32[]{:S(2)}) collective-permute-start(bf16[128,512]{1,0:T(8,128)(2,1)} %get-tuple-element.269), channel_id=1, source_target_pairs={{0,32},{32,64},{64,96},{96,128},{128,160},{160,192},{192,224},{224... | collective-permute-start | bytes 393224 | tf_op jit(solution)/shard_map/while/body/eval_jaxpr/ppermute | solution.py:32
  268.8 10.2 %collective-permute-start.1 = (f32[128,512]{1,0:T(8,128)}, f32[128,512]{1,0:T(8,128)S(1)}, u32[]{:S(2)}, u32[]{:S(2)}) collective-permute-start(f32[128,512]{1,0:T(8,128)} %get-tuple-element.270), channel_id=1, source_target_pairs={{0,32},{32,64},{64,96},{96,128},{128,160},{160,192},{192,224},{224... | collective-permute-start | bytes 786440 | tf_op jit(solution)/shard_map/while/body/eval_jaxpr/ppermute | solution.py:32
  270.1 8.9 %collective-permute-start = (bf16[128,512]{1,0:T(8,128)(2,1)}, bf16[128,512]{1,0:T(8,128)(2,1)S(1)}, u32[]{:S(2)}, u32[]{:S(2)}) collective-permute-start(bf16[128,512]{1,0:T(8,128)(2,1)} %get-tuple-element.269), channel_id=1, source_target_pairs={{0,32},{32,64},{64,96},{96,128},{128,160},{160,192},{192,224},{224... | collective-permute-start | bytes 393224 | tf_op jit(solution)/shard_map/while/body/eval_jaxpr/ppermute | solution.py:32
  282.4 10.5 %collective-permute-start.1 = (f32[128,512]{1,0:T(8,128)}, f32[128,512]{1,0:T(8,128)S(1)}, u32[]{:S(2)}, u32[]{:S(2)}) collective-permute-start(f32[128,512]{1,0:T(8,128)} %get-tuple-element.270), channel_id=1, source_target_pairs={{0,32},{32,64},{64,96},{96,128},{128,160},{160,192},{192,224},{224... | collective-permute-start | bytes 786440 | tf_op jit(solution)/shard_map/while/body/eval_jaxpr/ppermute | solution.py:32
  283.6 9.2 %collective-permute-start = (bf16[128,512]{1,0:T(8,128)(2,1)}, bf16[128,512]{1,0:T(8,128)(2,1)S(1)}, u32[]{:S(2)}, u32[]{:S(2)}) collective-permute-start(bf16[128,512]{1,0:T(8,128)(2,1)} %get-tuple-element.269), channel_id=1, source_target_pairs={{0,32},{32,64},{64,96},{96,128},{128,160},{160,192},{192,224},{224... | collective-permute-start | bytes 393224 | tf_op jit(solution)/shard_map/while/body/eval_jaxpr/ppermute | solution.py:32
  296.2 10.8 %collective-permute-start.1 = (f32[128,512]{1,0:T(8,128)}, f32[128,512]{1,0:T(8,128)S(1)}, u32[]{:S(2)}, u32[]{:S(2)}) collective-permute-start(f32[128,512]{1,0:T(8,128)} %get-tuple-element.270), channel_id=1, source_target_pairs={{0,32},{32,64},{64,96},{96,128},{128,160},{160,192},{192,224},{224... | collective-permute-start | bytes 786440 | tf_op jit(solution)/shard_map/while/body/eval_jaxpr/ppermute | solution.py:32
  297.5 9.5 %collective-permute-start = (bf16[128,512]{1,0:T(8,128)(2,1)}, bf16[128,512]{1,0:T(8,128)(2,1)S(1)}, u32[]{:S(2)}, u32[]{:S(2)}) collective-permute-start(bf16[128,512]{1,0:T(8,128)(2,1)} %get-tuple-element.269), channel_id=1, source_target_pairs={{0,32},{32,64},{64,96},{96,128},{128,160},{160,192},{192,224},{224... | collective-permute-start | bytes 393224 | tf_op jit(solution)/shard_map/while/body/eval_jaxpr/ppermute | solution.py:32
  310.3 12.1 %collective-permute-start.1 = (f32[128,512]{1,0:T(8,128)}, f32[128,512]{1,0:T(8,128)S(1)}, u32[]{:S(2)}, u32[]{:S(2)}) collective-permute-start(f32[128,512]{1,0:T(8,128)} %get-tuple-element.270), channel_id=1, source_target_pairs={{0,32},{32,64},{64,96},{96,128},{128,160},{160,192},{192,224},{224... | collective-permute-start | bytes 786440 | tf_op jit(solution)/shard_map/while/body/eval_jaxpr/ppermute | solution.py:32
  311.6 10.8 %collective-permute-start = (bf16[128,512]{1,0:T(8,128)(2,1)}, bf16[128,512]{1,0:T(8,128)(2,1)S(1)}, u32[]{:S(2)}, u32[]{:S(2)}) collective-permute-start(bf16[128,512]{1,0:T(8,128)(2,1)} %get-tuple-element.269), channel_id=1, source_target_pairs={{0,32},{32,64},{64,96},{96,128},{128,160},{160,192},{192,224},{224... | collective-permute-start | bytes 393224 | tf_op jit(solution)/shard_map/while/body/eval_jaxpr/ppermute | solution.py:32
  (3 other events, 5.3 us)
where the time goes:
time: 333 us; the launch traced here: 327 us
  waiting for transfers between devices  209 us (63%)
  starting transfers between devices  61.8 us (19%)
  local copies, waits for them, and re-layouts  25.4 us (8%)
  matrix products  20.4 us (6%)
  other arithmetic  8.38 us (3%)
    ppermute x42, waiting for transfers between devices, from_behind(): lax.ppermute(value, axis, [(source, source + steps) for source in range(i...  208 us
    ppermute x42, starting transfers between devices, from_behind(): lax.ppermute(value, axis, [(source, source + steps) for source in range(i...  54 us
    another operation x32, local copies, waits for them, and re-layouts  22.1 us
    dot_general x6, matrix products, gate_step(): jnp.dot(hidden, w_state, preferred_element_type=jnp.float32)  13.8 us
  transfers between devices with their start and end apart: 44, of which 22 were waited for; matrix products, arithmetic and copies ran while one was open for 0% of the time, Pallas kernels for 0%

commit v1 on v0

v1 whole, which is shorter than its diff:
```python
import functools

import jax
import jax.numpy as jnp
from jax import lax
from jax.experimental import pallas as pl
from jax.experimental.pallas import tpu as pltpu
from jax.sharding import PartitionSpec as P

MESH = pl.DeviceIdType.MESH
FORGET_BIAS = 2.0
GROUP = 4


def sigmoid(x):
    return 0.5 * jnp.tanh(0.5 * x) + 0.5


def kernel(
    snaps,
    verts,
    feat_hbm,
    adj_hbm,
    src_ref,
    dst_ref,
    count_ref,
    w_conv_hbm,
    b_conv_hbm,
    w_input_hbm,
    w_state_hbm,
    b_gates_hbm,
    out_ref,
    window,
    agg,
    agg_in,
    pre,
    cell,
    hid,
    adj_ref,
    w_conv,
    b_conv_ref,
    w_input,
    w_state,
    b_gates_ref,
    load_sem,
    halo_send,
    halo_recv,
    agg_send,
    agg_recv,
    hid_send,
    hid_recv,
):
    me = lax.axis_index("snap")
    own = lax.axis_index("vert")
    left, right = lax.rem(own + verts - 1, verts), lax.rem(own + 1, verts)
    slots, block, _ = adj_ref.shape
    row_blocks = window.shape[0] // 3
    rows = agg_in.shape[1]
    width = w_state.shape[0]

    loads = [
        pltpu.make_async_copy(feat_hbm, window.at[pl.ds(row_blocks, row_blocks)], load_sem.at[0]),
        pltpu.make_async_copy(adj_hbm, adj_ref, load_sem.at[1]),
        pltpu.make_async_copy(w_conv_hbm, w_conv, load_sem.at[2]),
        pltpu.make_async_copy(b_conv_hbm, b_conv_ref, load_sem.at[3]),
        pltpu.make_async_copy(w_input_hbm, w_input, load_sem.at[4]),
        pltpu.make_async_copy(b_gates_hbm, b_gates_ref, load_sem.at[5]),
        pltpu.make_async_copy(w_state_hbm, w_state, load_sem.at[6]),
    ]
    for load in loads:
        load.start()

    barrier = pltpu.get_barrier_semaphore()
    for near in (left, right):
        pl.semaphore_signal(barrier, inc=1, device_id={"vert": near}, device_id_type=MESH)

    def greet(k, carry):
        peer = lax.rem(me + k, snaps)
        pl.semaphore_signal(barrier, inc=1, device_id={"snap": peer}, device_id_type=MESH)
        return carry

    lax.fori_loop(1, snaps, greet, 0)
    pl.semaphore_wait(barrier, snaps + 1)
    loads[0].wait()

    middle = window.at[pl.ds(row_blocks, row_blocks)]
    halos = [
        pltpu.make_async_remote_copy(
            src_ref=middle,
            dst_ref=window.at[pl.ds(place * row_blocks, row_blocks)],
            send_sem=halo_send.at[i],
            recv_sem=halo_recv.at[i],
            device_id={"vert": near},
            device_id_type=MESH,
        )
        for i, (near, place) in enumerate(((right, 0), (left, 2)))
    ]
    for halo in halos:
        halo.start()
    for halo in halos:
        halo.wait()

    loads[1].wait()

    count = count_ref[0, 0]
    sums = [jnp.zeros((block, block), jnp.float32) for _ in range(row_blocks)]
    for slot in range(slots):
        place = jnp.clip(src_ref[0, slot] - (own - 1) * row_blocks, 0, 3 * row_blocks - 1)
        product = jnp.dot(adj_ref[slot], window[place], preferred_element_type=jnp.float32)
        target = dst_ref[0, slot]
        for r in range(row_blocks):
            taken = jnp.logical_and(target == r, slot < count)
            sums[r] = sums[r] + jnp.where(taken, product, 0.0)
    for r in range(row_blocks):
        agg[pl.ds(r * block, block), :] = sums[r].astype(agg.dtype)

    def agg_copy(k):
        peer = lax.rem(me + k, snaps)
        return pltpu.make_async_remote_copy(
            src_ref=agg.at[pl.ds(pl.multiple_of(peer * rows, rows), rows)],
            dst_ref=agg_in.at[me],
            send_sem=agg_send.at[k],
            recv_sem=agg_recv.at[me],
            device_id={"snap": peer},
            device_id_type=MESH,
        )

    def send_agg(k, carry):
        agg_copy(k).start()
        return carry

    lax.fori_loop(1, snaps, send_agg, 0)
    agg_in[me] = agg[pl.ds(pl.multiple_of(me * rows, rows), rows), :]

    def arrived(buffer, sem, index):
        return pltpu.make_async_remote_copy(
            src_ref=buffer,
            dst_ref=buffer,
            send_sem=sem.at[index],
            recv_sem=sem.at[index],
            device_id={"snap": lax.rem(me + 1, snaps)},
            device_id_type=MESH,
        )

    def hid_copy(step):
        return pltpu.make_async_remote_copy(
            src_ref=hid.at[step],
            dst_ref=out_ref.at[pl.ds(pl.multiple_of(me * rows, rows), rows)],
            send_sem=hid_send.at[step],
            recv_sem=hid_recv.at[me],
            device_id={"snap": step},
            device_id_type=MESH,
        )

    cell[...] = jnp.zeros_like(cell)
    for load in loads[2:]:
        load.wait()

    for first in range(0, snaps, GROUP):
        for t in range(first, first + GROUP):

            @pl.when(me != t)
            def _():
                arrived(agg_in.at[t], agg_recv, t).wait_recv()

        taken = agg_in[pl.ds(first, GROUP)].reshape(GROUP * rows, block)
        conv = jnp.dot(taken, w_conv[...], preferred_element_type=jnp.float32)
        conv = jnp.maximum(conv + b_conv_ref[...], 0.0).astype(jnp.bfloat16)
        for gate in range(4):
            columns = pl.ds(gate * width, width)
            part = jnp.dot(conv, w_input[:, columns], preferred_element_type=jnp.float32)
            part = part + b_gates_ref[:, columns]
            pre[:, :, columns] = part.reshape(GROUP, rows, width)

        def step_body(t, carry):
            local = t - first
            last = hid[lax.rem(t + snaps - 1, snaps)]
            if first == 0:
                last = jnp.where(t == 0, jnp.zeros_like(last), last)
            half = width // 2
            for c in range(2):
                gates = []
                for gate in range(4):
                    columns = pl.ds(gate * width + c * half, half)
                    gates.append(
                        pre[local, :, columns]
                        + jnp.dot(last, w_state[:, columns], preferred_element_type=jnp.float32)
                    )
                columns = pl.ds(c * half, half)
                new_cell = sigmoid(gates[1] + FORGET_BIAS) * cell[:, columns]
                new_cell = new_cell + sigmoid(gates[0]) * jnp.tanh(gates[2])
                cell[:, columns] = new_cell
                new_hidden = sigmoid(gates[3]) * jnp.tanh(new_cell)
                hid[t, :, columns] = new_hidden.astype(hid.dtype)

            @pl.when(me != t)
            def _():
                hid_copy(t).start()

            return carry

        lax.fori_loop(first, first + GROUP, step_body, 0)

    out_ref[pl.ds(pl.multiple_of(me * rows, rows), rows), :] = hid[me]

    def finish(k, carry):
        peer = lax.rem(me + k, snaps)
        agg_copy(k).wait_send()
        arrived(out_ref.at[pl.ds(pl.multiple_of(peer * rows, rows), rows)], hid_recv, peer).wait_recv()
        hid_copy(peer).wait_send()
        return carry

    lax.fori_loop(1, snaps, finish, 0)


def shards(
    snaps,
    verts,
    features,
    adjacency_tiles,
    src_block,
    dst_block,
    block_count,
    w_conv,
    b_conv,
    w_input,
    w_state,
    b_gates,
):
    _, vert_rows, feat = features.shape
    _, slots, block, _ = adjacency_tiles.shape
    out_width = w_conv.shape[1]
    width = w_state.shape[0]
    row_blocks = vert_rows // block
    rows = vert_rows // snaps
    vmem = pl.BlockSpec(memory_space=pltpu.VMEM)
    smem = pl.BlockSpec(memory_space=pltpu.SMEM)
    hbm = pl.BlockSpec(memory_space=pltpu.HBM)
    bf16, f32 = jnp.bfloat16, jnp.float32
    out = pl.pallas_call(
        functools.partial(kernel, snaps, verts),
        out_shape=jax.ShapeDtypeStruct((vert_rows, width), bf16),
        in_specs=[hbm, hbm, smem, smem, smem, hbm, hbm, hbm, hbm, hbm],
        out_specs=vmem,
        scratch_shapes=[
            pltpu.VMEM((3 * row_blocks, block, feat), bf16),
            pltpu.VMEM((vert_rows, feat), bf16),
            pltpu.VMEM((snaps, rows, feat), bf16),
            pltpu.VMEM((GROUP, rows, 4 * width), f32),
            pltpu.VMEM((rows, width), f32),
            pltpu.VMEM((snaps, rows, width), bf16),
            pltpu.VMEM((slots, block, block), bf16),
            pltpu.VMEM((feat, out_width), bf16),
            pltpu.VMEM((1, out_width), f32),
            pltpu.VMEM((out_width, 4 * width), bf16),
            pltpu.VMEM((width, 4 * width), bf16),
            pltpu.VMEM((1, 4 * width), f32),
            pltpu.SemaphoreType.DMA((7,)),
            pltpu.SemaphoreType.DMA((2,)),
            pltpu.SemaphoreType.DMA((2,)),
            pltpu.SemaphoreType.DMA((snaps,)),
            pltpu.SemaphoreType.DMA((snaps,)),
            pltpu.SemaphoreType.DMA((snaps,)),
            pltpu.SemaphoreType.DMA((snaps,)),
        ],
        compiler_params=pltpu.CompilerParams(
            collective_id=0, has_side_effects=True, vmem_limit_bytes=60 * 1024 * 1024
        ),
        cost_estimate=pl.CostEstimate(
            flops=4 * vert_rows * width * 4 * width, bytes_accessed=6_000_000, transcendentals=0
        ),
    )(
        features.reshape(row_blocks, block, feat),
        adjacency_tiles[0],
        src_block,
        dst_block,
        block_count,
        w_conv,
        b_conv[None],
        w_input,
        w_state,
        b_gates[None],
    )
    return out[None]


def solution(mesh):
    placed = (
        P("snap", "vert", None),
        P("snap", "vert", None, None),
        P("snap", "vert"),
        P("snap", "vert"),
        P("snap", "vert"),
        P(),
        P(),
        P(),
        P(),
        P(),
    )
    return jax.shard_map(
        functools.partial(shards, mesh.shape["snap"], mesh.shape["vert"]),
        mesh=mesh,
        in_specs=placed,
        out_specs=P("snap", "vert", None),
        check_vma=False,
    )
```

time: 333 us -> 75.4 us (0.23)
  the two profiles are of different devices: /device:TPU:504 before, /device:TPU:16 now
where the time goes in v1:
time: 75.4 us; the launch traced here: 75.2 us
  Pallas kernels  72.5 us (96%)
  local copies, waits for them, and re-layouts  2.06 us (3%)
    pallas_call x1, Pallas kernels, shards(): pl.pallas_call(functools.partial(kernel, snaps, verts), out_shape=jax.Sha...  72.5 us
    unnamed x1, local copies, waits for them, and re-layouts  2.06 us

profile of v1, /device:TPU:16, one launch (start us, length us, event | category | flops | bytes accessed | tf_op | source)
XLA Modules:
  0.0 75.2 jit_solution(11291837731571689294)
XLA Ops:
  0.7 72.5 %shard_map.100 = bf16[768,512]{1,0:T(8,128)(2,1)} custom-call(bf16[6,128,128]{2,1,0:T(8,128)(2,1)} %bitcast.7, bf16[12,128,128]{2,1,0:T(8,128)(2,1)} %bitcast.6, s32[1,12]{1,0:T(1,128)} %src_ref.1, s32[1,12]{1,0:T(1,128)} %dst_ref.1, s32[1,1]{1,0:T(1,128)S(6)} %copy.12.count_ref, bf16[128,512]{1,0:T(8,128)(2,1)} %w_conv_hbm.1, f32[1,512]{1,0:T(1,128)} %bitcast.9, ...), custom_call_target="tpu_custom_call" | custom-call | flops 3221225472 | bytes 6000000 | tf_op jit(solution)/shard_map/pallas_call | solution.py:240
  73.2 2.1 %copy.13 = bf16[1,768,512]{2,1,0:T(8,128)(2,1)} copy(bf16[1,768,512]{2,1,0:T(8,128)(2,1)} %bitcast.5) | data formatting | bytes 1572864

commit v2 on v1

--- a/solution.py
+++ b/solution.py
@@ -42,6 +42,7 @@
     w_input,
     w_state,
     b_gates_ref,
+    known,
     load_sem,
     halo_send,
     halo_recv,
@@ -73,14 +74,11 @@
     barrier = pltpu.get_barrier_semaphore()
     for near in (left, right):
         pl.semaphore_signal(barrier, inc=1, device_id={"vert": near}, device_id_type=MESH)
-
-    def greet(k, carry):
-        peer = lax.rem(me + k, snaps)
-        pl.semaphore_signal(barrier, inc=1, device_id={"snap": peer}, device_id_type=MESH)
-        return carry
-
-    lax.fori_loop(1, snaps, greet, 0)
-    pl.semaphore_wait(barrier, snaps + 1)
+    for near in (1, snaps - 1):
+        pl.semaphore_signal(
+            barrier, inc=1, device_id={"snap": lax.rem(me + near, snaps)}, device_id_type=MESH
+        )
+    pl.semaphore_wait(barrier, 4)
     loads[0].wait()
 
     middle = window.at[pl.ds(row_blocks, row_blocks)]
@@ -97,6 +95,18 @@
     ]
     for halo in halos:
         halo.start()
+
+    for turn, step in enumerate((1, 2, 4)):
+        for side, near in enumerate((step, snaps - step)):
+            pl.semaphore_signal(
+                known.at[turn, side],
+                inc=1,
+                device_id={"snap": lax.rem(me + near, snaps)},
+                device_id_type=MESH,
+            )
+        for side in range(2):
+            pl.semaphore_wait(known.at[turn, side], 1)
+
     for halo in halos:
         halo.wait()
 
@@ -255,6 +265,7 @@
             pltpu.VMEM((out_width, 4 * width), bf16),
             pltpu.VMEM((width, 4 * width), bf16),
             pltpu.VMEM((1, 4 * width), f32),
+            pltpu.SemaphoreType.REGULAR((3, 2)),
             pltpu.SemaphoreType.DMA((7,)),
             pltpu.SemaphoreType.DMA((2,)),
             pltpu.SemaphoreType.DMA((2,)),

time: 75.4 us -> 73.4 us (0.973)
  the two profiles are of different devices: /device:TPU:16 before, /device:TPU:22 now
where the time goes in v2:
time: 73.4 us; the launch traced here: 73.2 us
  Pallas kernels  70.5 us (96%)
  local copies, waits for them, and re-layouts  2.06 us (3%)
    pallas_call x1, Pallas kernels, shards(): pl.pallas_call(functools.partial(kernel, snaps, verts), out_shape=jax.Sha...  70.5 us
    unnamed x1, local copies, waits for them, and re-layouts  2.06 us

profile of v2, /device:TPU:22, one launch (start us, length us, event | category | flops | bytes accessed | tf_op | source)
XLA Modules:
  0.0 73.2 jit_solution(17477359003799177113)
XLA Ops:
  0.7 70.5 %shard_map.100 = bf16[768,512]{1,0:T(8,128)(2,1)} custom-call(bf16[6,128,128]{2,1,0:T(8,128)(2,1)} %bitcast.7, bf16[12,128,128]{2,1,0:T(8,128)(2,1)} %bitcast.6, s32[1,12]{1,0:T(1,128)} %src_ref.1, s32[1,12]{1,0:T(1,128)} %dst_ref.1, s32[1,1]{1,0:T(1,128)S(6)} %copy.12.count_ref, bf16[128,512]{1,0:T(8,128)(2,1)} %w_conv_hbm.1, f32[1,512]{1,0:T(1,128)} %bitcast.9, ...), custom_call_target="tpu_custom_call" | custom-call | flops 3221225472 | bytes 6000000 | tf_op jit(solution)/shard_map/pallas_call | solution.py:250
  71.2 2.1 %copy.13 = bf16[1,768,512]{2,1,0:T(8,128)(2,1)} copy(bf16[1,768,512]{2,1,0:T(8,128)(2,1)} %bitcast.5) | data formatting | bytes 1572864

commit v3 on v2

--- a/solution.py
+++ b/solution.py
@@ -10,6 +10,7 @@
 MESH = pl.DeviceIdType.MESH
 FORGET_BIAS = 2.0
 GROUP = 4
+PARTS = ((0, 16), (16, 32))
 
 
 def sigmoid(x):
@@ -71,14 +72,15 @@
     for load in loads:
         load.start()
 
+    def over_snap(step):
+        return {"snap": lax.rem(me + step, snaps)}
+
     barrier = pltpu.get_barrier_semaphore()
     for near in (left, right):
         pl.semaphore_signal(barrier, inc=1, device_id={"vert": near}, device_id_type=MESH)
-    for near in (1, snaps - 1):
-        pl.semaphore_signal(
-            barrier, inc=1, device_id={"snap": lax.rem(me + near, snaps)}, device_id_type=MESH
-        )
-    pl.semaphore_wait(barrier, 4)
+    for near in (2, snaps - 2, 1, snaps - 1):
+        pl.semaphore_signal(barrier, inc=1, device_id=over_snap(near), device_id_type=MESH)
+    pl.semaphore_wait(barrier, 6)
     loads[0].wait()
 
     middle = window.at[pl.ds(row_blocks, row_blocks)]
@@ -96,16 +98,19 @@
     for halo in halos:
         halo.start()
 
-    for turn, step in enumerate((1, 2, 4)):
+    def tell(turn, step):
         for side, near in enumerate((step, snaps - step)):
             pl.semaphore_signal(
-                known.at[turn, side],
-                inc=1,
-                device_id={"snap": lax.rem(me + near, snaps)},
-                device_id_type=MESH,
+                known.at[turn, side], inc=1, device_id=over_snap(near), device_id_type=MESH
             )
+
+    def hear(turn):
         for side in range(2):
             pl.semaphore_wait(known.at[turn, side], 1)
+
+    tell(0, 2)
+    hear(0)
+    tell(1, 4)
 
     for halo in halos:
         halo.wait()
@@ -124,40 +129,52 @@
     for r in range(row_blocks):
         agg[pl.ds(r * block, block), :] = sums[r].astype(agg.dtype)
 
-    def agg_copy(k):
+    def agg_copy(part, k):
+        start, size = PARTS[part]
         peer = lax.rem(me + k, snaps)
         return pltpu.make_async_remote_copy(
-            src_ref=agg.at[pl.ds(pl.multiple_of(peer * rows, rows), rows)],
-            dst_ref=agg_in.at[me],
-            send_sem=agg_send.at[k],
-            recv_sem=agg_recv.at[me],
+            src_ref=agg.at[pl.ds(pl.multiple_of(peer * rows + start, 16), size)],
+            dst_ref=agg_in.at[me, pl.ds(start, size)],
+            send_sem=agg_send.at[part, k],
+            recv_sem=agg_recv.at[part, me],
             device_id={"snap": peer},
             device_id_type=MESH,
         )
 
-    def send_agg(k, carry):
-        agg_copy(k).start()
-        return carry
-
-    lax.fori_loop(1, snaps, send_agg, 0)
+    def send_agg(part, first, last):
+        def both_ways(k, carry):
+            agg_copy(part, k).start()
+            agg_copy(part, snaps - k).start()
+            return carry
+
+        lax.fori_loop(first, last, both_ways, 0)
+
+    half_way = snaps // 2
+    send_agg(0, 1, 5)
+    hear(1)
+    send_agg(0, 5, half_way)
+    agg_copy(0, half_way).start()
+    send_agg(1, 1, half_way)
+    agg_copy(1, half_way).start()
     agg_in[me] = agg[pl.ds(pl.multiple_of(me * rows, rows), rows), :]
 
-    def arrived(buffer, sem, index):
+    def arrived(buffer, sem):
         return pltpu.make_async_remote_copy(
             src_ref=buffer,
             dst_ref=buffer,
-            send_sem=sem.at[index],
-            recv_sem=sem.at[index],
-            device_id={"snap": lax.rem(me + 1, snaps)},
+            send_sem=sem,
+            recv_sem=sem,
+            device_id=over_snap(1),
             device_id_type=MESH,
         )
 
-    def hid_copy(step):
+    def hid_copy(part, step):
+        start, size = PARTS[part]
         return pltpu.make_async_remote_copy(
-            src_ref=hid.at[step],
-            dst_ref=out_ref.at[pl.ds(pl.multiple_of(me * rows, rows), rows)],
-            send_sem=hid_send.at[step],
-            recv_sem=hid_recv.at[me],
+            src_ref=hid.at[step, pl.ds(start, size)],
+            dst_ref=out_ref.at[pl.ds(pl.multiple_of(me * rows + start, 16), size)],
+            send_sem=hid_send.at[part, step],
+            recv_sem=hid_recv.at[part, me],
             device_id={"snap": step},
             device_id_type=MESH,
         )
@@ -166,61 +183,66 @@
     for load in loads[2:]:
         load.wait()
 
-    for first in range(0, snaps, GROUP):
-        for t in range(first, first + GROUP):
-
-            @pl.when(me != t)
-            def _():
-                arrived(agg_in.at[t], agg_recv, t).wait_recv()
-
-        taken = agg_in[pl.ds(first, GROUP)].reshape(GROUP * rows, block)
-        conv = jnp.dot(taken, w_conv[...], preferred_element_type=jnp.float32)
-        conv = jnp.maximum(conv + b_conv_ref[...], 0.0).astype(jnp.bfloat16)
-        for gate in range(4):
-            columns = pl.ds(gate * width, width)
-            part = jnp.dot(conv, w_input[:, columns], preferred_element_type=jnp.float32)
-            part = part + b_gates_ref[:, columns]
-            pre[:, :, columns] = part.reshape(GROUP, rows, width)
-
-        def step_body(t, carry):
-            local = t - first
-            last = hid[lax.rem(t + snaps - 1, snaps)]
-            if first == 0:
-                last = jnp.where(t == 0, jnp.zeros_like(last), last)
-            half = width // 2
-            for c in range(2):
-                gates = []
-                for gate in range(4):
-                    columns = pl.ds(gate * width + c * half, half)
-                    gates.append(
-                        pre[local, :, columns]
-                        + jnp.dot(last, w_state[:, columns], preferred_element_type=jnp.float32)
-                    )
-                columns = pl.ds(c * half, half)
-                new_cell = sigmoid(gates[1] + FORGET_BIAS) * cell[:, columns]
-                new_cell = new_cell + sigmoid(gates[0]) * jnp.tanh(gates[2])
-                cell[:, columns] = new_cell
-                new_hidden = sigmoid(gates[3]) * jnp.tanh(new_cell)
-                hid[t, :, columns] = new_hidden.astype(hid.dtype)
-
-            @pl.when(me != t)
-            def _():
-                hid_copy(t).start()
-
-            return carry
-
-        lax.fori_loop(first, first + GROUP, step_body, 0)
+    def step_body(part, first, t, carry):
+        start, size = PARTS[part]
+        lines = pl.ds(start, size)
+        local = t - first
+        last = hid[lax.rem(t + snaps - 1, snaps), lines, :]
+        if first == 0:
+            last = jnp.where(t == 0, jnp.zeros_like(last), last)
+        half = width // 2
+        for c in range(2):
+            gates = []
+            for gate in range(4):
+                columns = pl.ds(gate * width + c * half, half)
+                gates.append(
+                    pre[pl.ds(pl.multiple_of(local * size, size), size), columns]
+                    + jnp.dot(last, w_state[:, columns], preferred_element_type=jnp.float32)
+                )
+            columns = pl.ds(c * half, half)
+            new_cell = sigmoid(gates[1] + FORGET_BIAS) * cell[lines, columns]
+            new_cell = new_cell + sigmoid(gates[0]) * jnp.tanh(gates[2])
+            cell[lines, columns] = new_cell
+            new_hidden = sigmoid(gates[3]) * jnp.tanh(new_cell)
+            hid[t, lines, columns] = new_hidden.astype(hid.dtype)
+
+        @pl.when(me != t)
+        def _():
+            hid_copy(part, t).start()
+
+        return carry
+
+    for part, (start, size) in enumerate(PARTS):
+        lines = pl.ds(start, size)
+        for first in range(0, snaps, GROUP):
+            for t in range(first, first + GROUP):
+
+                @pl.when(me != t)
+                def _():
+                    arrived(agg_in.at[t, lines], agg_recv.at[part, t]).wait_recv()
+
+            taken = agg_in[pl.ds(first, GROUP), lines, :].reshape(GROUP * size, block)
+            conv = jnp.dot(taken, w_conv[...], preferred_element_type=jnp.float32)
+            conv = jnp.maximum(conv + b_conv_ref[...], 0.0).astype(jnp.bfloat16)
+            for gate in range(4):
+                columns = pl.ds(gate * width, width)
+                product = jnp.dot(conv, w_input[:, columns], preferred_element_type=jnp.float32)
+                pre[pl.ds(0, GROUP * size), columns] = product + b_gates_ref[:, columns]
+            lax.fori_loop(first, first + GROUP, functools.partial(step_body, part, first), 0)
 
     out_ref[pl.ds(pl.multiple_of(me * rows, rows), rows), :] = hid[me]
 
-    def finish(k, carry):
+    def finish(part, k, carry):
+        start, size = PARTS[part]
         peer = lax.rem(me + k, snaps)
-        agg_copy(k).wait_send()
-        arrived(out_ref.at[pl.ds(pl.multiple_of(peer * rows, rows), rows)], hid_recv, peer).wait_recv()
-        hid_copy(peer).wait_send()
+        agg_copy(part, k).wait_send()
+        lines = pl.ds(pl.multiple_of(peer * rows + start, 16), size)
+        arrived(out_ref.at[lines], hid_recv.at[part, peer]).wait_recv()
+        hid_copy(part, peer).wait_send()
         return carry
 
-    lax.fori_loop(1, snaps, finish, 0)
+    for part in range(len(PARTS)):
+        lax.fori_loop(1, snaps, functools.partial(finish, part), 0)
 
 
 def shards(
@@ -256,7 +278,7 @@
             pltpu.VMEM((3 * row_blocks, block, feat), bf16),
             pltpu.VMEM((vert_rows, feat), bf16),
             pltpu.VMEM((snaps, rows, feat), bf16),
-            pltpu.VMEM((GROUP, rows, 4 * width), f32),
+            pltpu.VMEM((GROUP * rows, 4 * width), f32),
             pltpu.VMEM((rows, width), f32),
             pltpu.VMEM((snaps, rows, width), bf16),
             pltpu.VMEM((slots, block, block), bf16),
@@ -265,14 +287,14 @@
             pltpu.VMEM((out_width, 4 * width), bf16),
             pltpu.VMEM((width, 4 * width), bf16),
             pltpu.VMEM((1, 4 * width), f32),
-            pltpu.SemaphoreType.REGULAR((3, 2)),
+            pltpu.SemaphoreType.REGULAR((2, 2)),
             pltpu.SemaphoreType.DMA((7,)),
             pltpu.SemaphoreType.DMA((2,)),
             pltpu.SemaphoreType.DMA((2,)),
-            pltpu.SemaphoreType.DMA((snaps,)),
-            pltpu.SemaphoreType.DMA((snaps,)),
-            pltpu.SemaphoreType.DMA((snaps,)),
-            pltpu.SemaphoreType.DMA((snaps,)),
+            pltpu.SemaphoreType.DMA((len(PARTS), snaps)),
+            pltpu.SemaphoreType.DMA((len(PARTS), snaps)),
+            pltpu.SemaphoreType.DMA((len(PARTS), snaps)),
+            pltpu.SemaphoreType.DMA((len(PARTS), snaps)),
         ],
         compiler_params=pltpu.CompilerParams(
             collective_id=0, has_side_effects=True, vmem_limit_bytes=60 * 1024 * 1024

time: 73.4 us -> 67 us (0.913)
  the two profiles are of different devices: /device:TPU:22 before, /device:TPU:504 now
where the time goes in v3:
time: 67 us; the launch traced here: 65.7 us
  Pallas kernels  63 us (94%)
  local copies, waits for them, and re-layouts  2.06 us (3%)
    pallas_call x1, Pallas kernels, shards(): pl.pallas_call(functools.partial(kernel, snaps, verts), out_shape=jax.Sha...  63 us
    unnamed x1, local copies, waits for them, and re-layouts  2.06 us

profile of v3, /device:TPU:504, one launch (start us, length us, event | category | flops | bytes accessed | tf_op | source)
XLA Modules:
  0.0 65.7 jit_solution(12794397108303618354)
XLA Ops:
  0.7 63.0 %shard_map.100 = bf16[768,512]{1,0:T(8,128)(2,1)} custom-call(bf16[6,128,128]{2,1,0:T(8,128)(2,1)} %bitcast.7, bf16[12,128,128]{2,1,0:T(8,128)(2,1)} %bitcast.6, s32[1,12]{1,0:T(1,128)} %src_ref.1, s32[1,12]{1,0:T(1,128)} %dst_ref.1, s32[1,1]{1,0:T(1,128)S(6)} %copy.12.count_ref, bf16[128,512]{1,0:T(8,128)(2,1)} %w_conv_hbm.1, f32[1,512]{1,0:T(1,128)} %bitcast.9, ...), custom_call_target="tpu_custom_call" | custom-call | flops 3221225472 | bytes 6000000 | tf_op jit(solution)/shard_map/pallas_call | solution.py:272
  63.6 2.1 %copy.13 = bf16[1,768,512]{2,1,0:T(8,128)(2,1)} copy(bf16[1,768,512]{2,1,0:T(8,128)(2,1)} %bitcast.5) | data formatting | bytes 1572864

commit v4 on v3

--- a/solution.py
+++ b/solution.py
@@ -230,7 +230,11 @@
                 pre[pl.ds(0, GROUP * size), columns] = product + b_gates_ref[:, columns]
             lax.fori_loop(first, first + GROUP, functools.partial(step_body, part, first), 0)
 
-    out_ref[pl.ds(pl.multiple_of(me * rows, rows), rows), :] = hid[me]
+    kept = pltpu.make_async_copy(
+        hid.at[me], out_ref.at[pl.ds(pl.multiple_of(me * rows, rows), rows)], load_sem.at[0]
+    )
+    kept.start()
+    kept.wait()
 
     def finish(part, k, carry):
         start, size = PARTS[part]
@@ -273,7 +277,7 @@
         functools.partial(kernel, snaps, verts),
         out_shape=jax.ShapeDtypeStruct((vert_rows, width), bf16),
         in_specs=[hbm, hbm, smem, smem, smem, hbm, hbm, hbm, hbm, hbm],
-        out_specs=vmem,
+        out_specs=hbm,
         scratch_shapes=[
             pltpu.VMEM((3 * row_blocks, block, feat), bf16),
             pltpu.VMEM((vert_rows, feat), bf16),

time: 67 us -> 66.2 us (0.988)
  Pallas kernels: 63 us -> 62.2 us
    pallas_call x1, Pallas kernels: 63 us -> 62.2 us  [shards(): pl.pallas_call(functools.partial(kernel, snaps, verts), out_shape=jax.Sha...]
where the time goes in v4:
time: 66.2 us; the launch traced here: 64.9 us
  Pallas kernels  62.2 us (94%)
  local copies, waits for them, and re-layouts  2.06 us (3%)
    pallas_call x1, Pallas kernels, shards(): pl.pallas_call(functools.partial(kernel, snaps, verts), out_shape=jax.Sha...  62.2 us
    unnamed x1, local copies, waits for them, and re-layouts  2.06 us

profile of v4, /device:TPU:504, one launch (start us, length us, event | category | flops | bytes accessed | tf_op | source)
XLA Modules:
  0.0 64.9 jit_solution(1722114740245269040)
XLA Ops:
  0.7 62.2 %shard_map.100 = bf16[768,512]{1,0:T(8,128)(2,1)} custom-call(bf16[6,128,128]{2,1,0:T(8,128)(2,1)} %bitcast.7, bf16[12,128,128]{2,1,0:T(8,128)(2,1)} %bitcast.6, s32[1,12]{1,0:T(1,128)} %src_ref.1, s32[1,12]{1,0:T(1,128)} %dst_ref.1, s32[1,1]{1,0:T(1,128)S(6)} %copy.12.count_ref, bf16[128,512]{1,0:T(8,128)(2,1)} %w_conv_hbm.1, f32[1,512]{1,0:T(1,128)} %bitcast.9, ...), custom_call_target="tpu_custom_call" | custom-call | flops 3221225472 | bytes 6000000 | tf_op jit(solution)/shard_map/pallas_call | solution.py:276
  62.9 2.1 %copy.13 = bf16[1,768,512]{2,1,0:T(8,128)(2,1)} copy(bf16[1,768,512]{2,1,0:T(8,128)(2,1)} %bitcast.5) | data formatting | bytes 1572864

commit v5 on v4

--- a/solution.py
+++ b/solution.py
@@ -78,9 +78,9 @@
     barrier = pltpu.get_barrier_semaphore()
     for near in (left, right):
         pl.semaphore_signal(barrier, inc=1, device_id={"vert": near}, device_id_type=MESH)
-    for near in (2, snaps - 2, 1, snaps - 1):
+    for near in (4, snaps - 4, 3, snaps - 3, 2, snaps - 2, 1, snaps - 1):
         pl.semaphore_signal(barrier, inc=1, device_id=over_snap(near), device_id_type=MESH)
-    pl.semaphore_wait(barrier, 6)
+    pl.semaphore_wait(barrier, 10)
     loads[0].wait()
 
     middle = window.at[pl.ds(row_blocks, row_blocks)]
@@ -108,9 +108,7 @@
         for side in range(2):
             pl.semaphore_wait(known.at[turn, side], 1)
 
-    tell(0, 2)
-    hear(0)
-    tell(1, 4)
+    tell(0, 4)
 
     for halo in halos:
         halo.wait()
@@ -151,7 +149,7 @@
 
     half_way = snaps // 2
     send_agg(0, 1, 5)
-    hear(1)
+    hear(0)
     send_agg(0, 5, half_way)
     agg_copy(0, half_way).start()
     send_agg(1, 1, half_way)
@@ -291,7 +289,7 @@
             pltpu.VMEM((out_width, 4 * width), bf16),
             pltpu.VMEM((width, 4 * width), bf16),
             pltpu.VMEM((1, 4 * width), f32),
-            pltpu.SemaphoreType.REGULAR((2, 2)),
+            pltpu.SemaphoreType.REGULAR((1, 2)),
             pltpu.SemaphoreType.DMA((7,)),
             pltpu.SemaphoreType.DMA((2,)),
             pltpu.SemaphoreType.DMA((2,)),

time: 66.2 us -> 65.4 us (0.988); the launches traced: 64.9 us -> 65.2 us
  no operation moved by 1% of the time
where the time goes in v5:
time: 65.4 us; the launch traced here: 65.2 us
  Pallas kernels  62.5 us (96%)
  local copies, waits for them, and re-layouts  2.06 us (3%)
  between operations  0.66 us (1%)
    pallas_call x1, Pallas kernels, shards(): pl.pallas_call(functools.partial(kernel, snaps, verts), out_shape=jax.Sha...  62.5 us
    unnamed x1, local copies, waits for them, and re-layouts  2.06 us

profile of v5, /device:TPU:504, one launch (start us, length us, event | category | flops | bytes accessed | tf_op | source)
XLA Modules:
  0.0 65.2 jit_solution(2985010665516178309)
XLA Ops:
  0.7 62.5 %shard_map.100 = bf16[768,512]{1,0:T(8,128)(2,1)} custom-call(bf16[6,128,128]{2,1,0:T(8,128)(2,1)} %bitcast.7, bf16[12,128,128]{2,1,0:T(8,128)(2,1)} %bitcast.6, s32[1,12]{1,0:T(1,128)} %src_ref.1, s32[1,12]{1,0:T(1,128)} %dst_ref.1, s32[1,1]{1,0:T(1,128)S(6)} %copy.12.count_ref, bf16[128,512]{1,0:T(8,128)(2,1)} %w_conv_hbm.1, f32[1,512]{1,0:T(1,128)} %bitcast.9, ...), custom_call_target="tpu_custom_call" | custom-call | flops 3221225472 | bytes 6000000 | tf_op jit(solution)/shard_map/pallas_call | solution.py:274
  63.2 2.1 %copy.13 = bf16[1,768,512]{2,1,0:T(8,128)(2,1)} copy(bf16[1,768,512]{2,1,0:T(8,128)(2,1)} %bitcast.5) | data formatting | bytes 1572864
